TPU v7x, 32 devices: a whole 2x2x4 slice. The times are simulated.
32 devices in a mesh: section: 2 (over x), slab: 16 (over z, y, core).
Axes of the slice: x: 2, y: 2, z: 4, core: 2. Of those that a mesh axis runs over, the one named last changes fastest.
Arguments:
- fields: bfloat16 [2, 4, 32, 128, 128], P('section', None, 'slab'), may hold values from -6 to 6
- lift_weight: bfloat16 [4, 32], replicated, may hold values from -3 to 3
- lift_bias: bfloat16 [32], replicated, may hold values from -3 to 3
- spectral_weight: bfloat16 [2, 2, 32, 32, 16384], P(None, None, None, 'section', 'slab'), may hold values from -0.75 to 0.75
- bypass_weight: bfloat16 [2, 32, 32], replicated, may hold values from -1 to 1
- bypass_bias: bfloat16 [2, 32], replicated, may hold values from -3 to 3
Outputs:
- features: bfloat16 [2, 32, 32, 128, 128], P('section', None, 'slab')
All inputs are finite; a program needn't handle non-finite values.
Results may differ from a plain program's by a relative error of at most 0.015.
Values may be sent and summed in bfloat16 or wider, within the bound.
A program may use at most 64 MiB of HBM per device.

v0:
```python
import functools
import math

import jax
import jax.numpy as jnp
import ml_dtypes
import numpy as np
from jax import lax
from jax.experimental import pallas as pl
from jax.experimental.pallas import tpu as pltpu
from jax.sharding import PartitionSpec as P

K = 16
LAYERS = 2


def signed_list(count):
    base = jnp.arange(2 * count, dtype=jnp.int32)
    return jnp.where(base < count, base, base - 2 * count)


def tables(freqs, length, span):
    freq = (freqs % length)[:, None]
    where = jnp.arange(span, dtype=jnp.int32)[None, :]
    phase = (freq * where % length).astype(jnp.float32) * (2.0 * math.pi / length)
    return (jnp.cos(phase).astype(jnp.bfloat16), jnp.sin(phase).astype(jnp.bfloat16))


def forward_pair(freqs, length):
    cosine, sine = tables(freqs, length, length)
    return jnp.concatenate([cosine, -sine], axis=0).T


def inverse_planes(mixed, cosine, sine):
    plain = jnp.einsum("mcrjk,kz->mcrjz", mixed, cosine, preferred_element_type=jnp.float32)
    skewed = jnp.einsum("mcrjk,kz->mcrjz", mixed, sine, preferred_element_type=jnp.float32)
    joined = jnp.stack([plain[:, :, 0] - skewed[:, :, 1], skewed[:, :, 0] + plain[:, :, 1]], 2)
    return (joined * 0.25).astype(jnp.bfloat16)


def on_device(fields, lift_weight, lift_bias, spectral_weight, bypass_weight, bypass_bias):
    slabs = lax.axis_size("slab")
    batch, inputs, depth, rows_x, rows_y = fields.shape
    width = lift_weight.shape[1]
    whole_z = depth * slabs
    half = 2 * K
    modes_xy = half * half
    owned = modes_xy // slabs
    place = lax.axis_index("slab")
    hidden = (
        jnp.einsum("mczxy,cd->mdzxy", fields, lift_weight, preferred_element_type=jnp.float32)
        + lift_bias.astype(jnp.float32)[None, :, None, None, None]
    ).astype(jnp.bfloat16)
    xy_list = signed_list(K)
    z_list = jnp.arange(K, dtype=jnp.int32)
    table_y = forward_pair(xy_list, rows_y)
    table_x = forward_pair(xy_list, rows_x)
    table_z = forward_pair(z_list, whole_z)
    doubling = jnp.where(z_list == 0, 1.0, 2.0).astype(jnp.bfloat16)[:, None]
    cos_z, sin_z = tables(z_list, whole_z, whole_z)
    cos_z = cos_z * doubling
    sin_z = sin_z * doubling
    cos_x, sin_x = tables(xy_list, rows_x, rows_x)
    cos_y, sin_y = tables(xy_list, rows_y, rows_y)
    back_y = jnp.concatenate([cos_y, -sin_y], axis=0)
    combined_x = jnp.stack([jnp.stack([cos_x, sin_x], 1), jnp.stack([-sin_x, cos_x], 1)], 0)
    index_modes = place * (owned * K) + jnp.arange(owned * K, dtype=jnp.int32)
    keep = (index_modes != 0).astype(jnp.float32).reshape(owned, K)
    scale_z = 1.0 / math.sqrt(whole_z)
    highest = lax.Precision.HIGHEST
    for layer in range(LAYERS):
        spectral = lax.all_gather(spectral_weight[layer], "section", axis=2, tiled=True)
        along_y = (
            jnp.dot(hidden, table_y, preferred_element_type=jnp.float32) / math.sqrt(rows_y)
        ).astype(jnp.bfloat16)
        both = jnp.einsum("mczxq,xp->mczpq", along_y, table_x, preferred_element_type=jnp.float32)
        spec_real = both[..., :half, :half] - both[..., half:, half:]
        spec_imag = both[..., :half, half:] + both[..., half:, :half]
        spectrum = (jnp.stack([spec_real, spec_imag], 2) / math.sqrt(rows_x)).astype(jnp.bfloat16)
        spectrum = spectrum.reshape(batch, width, 2, depth, modes_xy).transpose(0, 1, 2, 4, 3)
        gathered = lax.all_to_all(spectrum, "slab", split_axis=3, concat_axis=4, tiled=True)
        along_z = jnp.einsum(
            "mcrjz,zq->mcrjq", gathered, table_z, preferred_element_type=jnp.float32
        )
        mode_real = (along_z[:, :, 0, :, :K] - along_z[:, :, 1, :, K:]) * scale_z * keep
        mode_imag = (along_z[:, :, 1, :, :K] + along_z[:, :, 0, :, K:]) * scale_z * keep
        weights = spectral.astype(jnp.float32).reshape(2, width, width, owned, K)
        mixed_real = jnp.einsum(
            "mijk,iojk->mojk", mode_real, weights[0], precision=highest
        ) - jnp.einsum("mijk,iojk->mojk", mode_imag, weights[1], precision=highest)
        mixed_imag = jnp.einsum(
            "mijk,iojk->mojk", mode_imag, weights[0], precision=highest
        ) + jnp.einsum("mijk,iojk->mojk", mode_real, weights[1], precision=highest)
        mixed = jnp.stack([mixed_real, mixed_imag], 2).astype(jnp.bfloat16)
        every_plane = inverse_planes(mixed, cos_z, sin_z)
        planes_back = lax.all_to_all(every_plane, "slab", split_axis=4, concat_axis=3, tiled=True)
        grid = planes_back.reshape(batch, width, 2, half, half, depth)
        along_x = (
            jnp.einsum("mcrpqz,rpsx->mczxsq", grid, combined_x, preferred_element_type=jnp.float32)
            * 0.125
        ).astype(jnp.bfloat16)
        along_x = along_x.reshape(batch, width, depth, rows_x, 2 * half)
        spectral_field = jnp.dot(along_x, back_y, preferred_element_type=jnp.float32) * 0.125
        bypassed = (
            jnp.einsum(
                "mczxy,co->mozxy", hidden, bypass_weight[layer], preferred_element_type=jnp.float32
            )
            + bypass_bias[layer].astype(jnp.float32)[None, :, None, None, None]
        )
        hidden = jax.nn.gelu(bypassed + spectral_field, approximate=True).astype(jnp.bfloat16)
    return hidden


BF = ml_dtypes.bfloat16


def host_tables(freqs, length):
    phase = (freqs[:, None] * np.arange(length)[None, :]) % length * (2.0 * math.pi / length)
    return (
        np.cos(phase).astype(BF).astype(np.float64),
        np.sin(phase).astype(BF).astype(np.float64),
    )


def constants(slabs, depth, nx, ny, width):
    whole_z = slabs * depth
    half = 2 * K
    lift = half // slabs
    groups = width // 4
    signed = np.where(np.arange(half) < K, np.arange(half), np.arange(half) - half)
    cy, sy = host_tables(signed, ny)
    cx, sx = host_tables(signed, nx)
    cz, sz = host_tables(np.arange(K), whole_z)
    eye4 = np.eye(4)
    fwd_y = np.concatenate([np.kron(eye4, cy.T), np.kron(eye4, -sy.T)], 1)
    fwd_x = np.block([[cx, sx], [-sx, cx]])
    rows = groups * depth * 2
    order = np.arange(rows * half).reshape(rows, slabs, lift).transpose(1, 0, 2).ravel()
    spread = np.eye(rows * half)[order]
    collect = spread.T
    pair = np.stack([np.stack([cz, sz], 1), np.stack([-sz, cz], 1)], 0)
    pair = pair.reshape(2, K, 2, slabs, depth)
    fwd_z = np.einsum("akbsd,gh,pq->gpakshdbq", pair, np.eye(groups), np.eye(lift))
    fwd_z = fwd_z.reshape(groups * lift * 2 * K, slabs * rows * lift)
    tile = np.kron(np.eye(8), np.tile(np.eye(K), (1, half)))
    total = np.kron(np.eye(width), np.ones((1, half)))
    double = np.where(np.arange(K) == 0, 1.0, 2.0)[:, None]
    dz, ez = cz * double, sz * double
    back = np.stack([np.stack([dz, -ez], 0), np.stack([ez, dz], 0)], 0)
    back = back.reshape(2, 2, K, slabs, depth).transpose(3, 4, 0, 1, 2)
    back_z = np.broadcast_to(back[:, :, :, :, None, :], (slabs, depth, 2, 2, half, K))
    back_z = back_z.reshape(whole_z * 2, 2 * half * K).T
    order = np.arange(groups * lift * whole_z * 2).reshape(groups, lift, slabs, depth, 2)
    order = order.transpose(2, 0, 3, 4, 1).ravel()
    leave = np.eye(order.size)[order]
    back_x = np.block([[cx.T, -sx.T], [sx.T, cx.T]])
    back_y = np.concatenate([np.kron(eye4, cy), np.kron(eye4, -sy)], 0)
    named = dict(
        fwd_y=fwd_y, fwd_x=fwd_x, spread=spread, collect=collect, fwd_z=fwd_z, tile=tile,
        total=total, expand=total.T, back_z=back_z, leave=leave, back_x=back_x, back_y=back_y,
    )
    return {name: np.ascontiguousarray(value).astype(BF) for name, value in named.items()}


def mm(a, b):
    return jnp.dot(a, b, preferred_element_type=jnp.float32)


def mask_of(half):
    row = lax.broadcasted_iota(jnp.int32, (4 * half, half * K), 0) % half
    column = lax.broadcasted_iota(jnp.int32, (4 * half, half * K), 1) // K
    return row == column


def lift_body(fields, kron, bias, hidden):
    width, depth, nx, ny = hidden.shape
    for z in range(depth):
        for g in range(nx // 16):
            block = fields[:, z, g * 16 : g * 16 + 16, :].reshape(-1, ny)
            value = mm(kron[...], block).reshape(width, 16, ny) + bias[...]
            hidden[:, z, g * 16 : g * 16 + 16, :] = value.astype(jnp.bfloat16)


def forward_body(hidden, fwd_y, fwd_x, spread, local, out):
    width, depth, nx, ny = hidden.shape
    for g in range(width // 4):
        for z in range(depth):
            block = jnp.concatenate([hidden[4 * g + c, z] for c in range(4)], axis=1)
            along = (mm(block, fwd_y[...]) * (1.0 / math.sqrt(ny))).astype(jnp.bfloat16)
            lanes = along.shape[1] // 2
            along = jnp.concatenate([along[:, :lanes], along[:, lanes:]], axis=0)
            spec = mm(fwd_x[...], along) * (1.0 / math.sqrt(nx))
            at = (g * depth + z) * spec.shape[0]
            local[at : at + spec.shape[0], :] = spec.astype(jnp.bfloat16)
    out[...] = mm(spread[...], local[...]).astype(jnp.bfloat16)


def modes_body(place, got, fwd_z, tile, total, modes, held, scale):
    half = 2 * K
    lanes = half * K
    width = modes.shape[1]
    lift = modes.shape[2] // lanes
    mask = mask_of(half)
    flat = (mm(fwd_z[...], got[...]) * scale).T.astype(jnp.bfloat16)
    per = lift * 2
    for b in range(flat.shape[1] // 128):
        wide = mm(flat[:, b * 128 : b * 128 + 128], tile[...])
        for e in range(8):
            g, pr = divmod(b * 8 + e, per)
            piece = jnp.where(mask, wide[:, e * lanes : (e + 1) * lanes], 0.0)
            held[pr, g * 128 : g * 128 + 128, :] = piece.astype(jnp.bfloat16)
    for p in range(lift):
        for r in range(2):
            value = mm(total[...], held[p * 2 + r])
            if p == 0:
                lane = lax.broadcasted_iota(jnp.int32, value.shape, 1)
                value = jnp.where(lane + place == 0, 0.0, value)
            modes[r, :, p * lanes : (p + 1) * lanes] = value.astype(jnp.bfloat16)


def mix_body(modes, weights, mixed):
    variants, _, width, lanes = modes.shape
    step = 256
    for b in range(lanes // step):
        at = slice(b * step, (b + 1) * step)
        rows = [[modes[m, r, :, at].astype(jnp.float32) for r in range(2)] for m in range(variants)]
        sums = [[0.0, 0.0] for _ in range(variants)]
        for i in range(width):
            wr = weights[0, i, :, at].astype(jnp.float32)
            wi = weights[1, i, :, at].astype(jnp.float32)
            for m in range(variants):
                real, imag = rows[m][0][i : i + 1], rows[m][1][i : i + 1]
                sums[m][0] += real * wr - imag * wi
                sums[m][1] += imag * wr + real * wi
        for m in range(variants):
            for r in range(2):
                mixed[m, r, :, at] = sums[m][r].astype(jnp.bfloat16)


def planes_body(mixed, expand, back_z, leave, out, local):
    half = 2 * K
    lanes = half * K
    mask = mask_of(half)
    sections = mixed.shape[0]
    lift = mixed.shape[3] // lanes
    groups = expand.shape[0] // 128
    many = back_z.shape[1]
    wholes = [
        jnp.concatenate([mixed[s, r] for s in range(sections)], axis=0) for r in range(2)
    ]
    for g in range(groups):
        values = []
        for p in range(lift):
            pieces = []
            for r in range(2):
                part = wholes[r][:, p * lanes : (p + 1) * lanes]
                wide = mm(expand[g * 128 : g * 128 + 128, :], part)
                pieces.append(jnp.where(mask, wide, 0.0).astype(jnp.bfloat16))
            values.append(mm(jnp.concatenate(pieces, axis=1), back_z[...]) * 0.25)
        value = jnp.concatenate(values, axis=1).T
        local[g * lift * many : (g + 1) * lift * many, :] = value.astype(jnp.bfloat16)
    out[...] = mm(leave[...], local[...]).astype(jnp.bfloat16)


def bypass_body(hidden, kron, bias, direct):
    width, depth, nx, ny = hidden.shape
    for z in range(depth):
        for g in range(nx // 16):
            block = hidden[:, z, g * 16 : g * 16 + 16, :].reshape(-1, ny)
            value = mm(kron[...], block).reshape(width, 16, ny) + bias[...]
            direct[:, z, g * 16 : g * 16 + 16, :] = value


def backward_body(got, direct, collect, back_x, back_y, local, out):
    width, depth, nx, ny = out.shape
    many = back_x.shape[1]
    local[...] = mm(collect[...], got[...]).astype(jnp.bfloat16)
    for g in range(width // 4):
        for z in range(depth):
            at = (g * depth + z) * many
            along = (mm(back_x[...], local[at : at + many, :]) * 0.125).astype(jnp.bfloat16)
            along = jnp.concatenate([along[:nx], along[nx:]], axis=1)
            field = mm(along, back_y[...]) * 0.125
            for c in range(4):
                value = direct[4 * g + c, z] + field[:, c * ny : (c + 1) * ny]
                inner = value * (0.7978845608028654 + 0.035677408136300125 * (value * value))
                value = 0.5 * value * (1.0 + jnp.tanh(inner))
                out[4 * g + c, z] = value.astype(jnp.bfloat16)


def widen(weight, copies):
    ins, outs = weight.shape

    def rep(n):
        row = lax.broadcasted_iota(jnp.int32, (n * copies, n), 0) // copies
        column = lax.broadcasted_iota(jnp.int32, (n * copies, n), 1)
        return (row == column).astype(jnp.bfloat16)

    def last(a, b):
        return lax.dot_general(a, b, (((1,), (1,)), ((), ())), preferred_element_type=jnp.float32)

    tall = last(rep(outs), weight).astype(jnp.bfloat16)
    wide = last(tall, rep(ins))
    row = lax.broadcasted_iota(jnp.int32, wide.shape, 0) % copies
    column = lax.broadcasted_iota(jnp.int32, wide.shape, 1) % copies
    return jnp.where(row == column, wide, 0.0).astype(jnp.bfloat16)


def start_kernel(fields, lift_weight, lift_bias, fwd_y, fwd_x, spread, hidden, out, kron, local):
    kron[...] = widen(lift_weight[...], 16)
    lift_body(fields, kron, lift_bias, hidden)
    forward_body(hidden, fwd_y, fwd_x, spread, local, out)


def modes_kernel(scale, got, fwd_z, tile, total, modes, held):
    place = lax.axis_index("slab")
    modes_body(place, got, fwd_z, tile, total, modes, held, scale)


def layer_kernel(
    got, hidden, weight, bias, collect, back_x, back_y, fwd_y, fwd_x, spread,
    new, out, kron, direct, local,
):
    kron[...] = widen(weight[...], 16)
    bypass_body(hidden, kron, bias, direct)
    backward_body(got, direct, collect, back_x, back_y, local, new)
    forward_body(new, fwd_y, fwd_x, spread, local, out)


def last_kernel(got, hidden, weight, bias, collect, back_x, back_y, new, kron, direct, local):
    kron[...] = widen(weight[...], 16)
    bypass_body(hidden, kron, bias, direct)
    backward_body(got, direct, collect, back_x, back_y, local, new)


def call(kernel, outs, scratch, *args):
    return pl.pallas_call(
        kernel,
        out_shape=outs,
        in_specs=[pl.BlockSpec(memory_space=pltpu.VMEM)] * len(args),
        out_specs=jax.tree.map(lambda _: pl.BlockSpec(memory_space=pltpu.VMEM), outs),
        scratch_shapes=scratch,
        compiler_params=pltpu.CompilerParams(vmem_limit_bytes=50 * 1024 * 1024),
    )(*args)


def on_device_fast(fields, lift_weight, lift_bias, spectral_weight, bypass_weight, bypass_bias):
    slabs, sections = lax.axis_size("slab"), lax.axis_size("section")
    _, inputs, depth, nx, ny = fields.shape
    width = lift_weight.shape[1]
    half = 2 * K
    owned = half * half // slabs
    bf = jnp.bfloat16
    t = constants(slabs, depth, nx, ny, width)
    t = {name: jnp.asarray(value) for name, value in t.items()}
    rows = width // 4 * depth * 2 * half

    def spread_bias(b):
        return jnp.broadcast_to(b.astype(jnp.float32)[..., None, None], b.shape + (1, ny))

    kron = pltpu.VMEM((width * 16, width * 16), bf)
    local = pltpu.VMEM((rows, 128), bf)
    spec = jax.ShapeDtypeStruct((rows, 128), bf)
    hid = jax.ShapeDtypeStruct((width, depth, nx, ny), bf)
    direct = pltpu.VMEM((width, depth, nx, ny), jnp.float32)
    bias = spread_bias(bypass_bias)
    hidden, out = call(
        start_kernel, (hid, spec), [pltpu.VMEM((width * 16, inputs * 16), bf), local],
        fields[0], lift_weight, spread_bias(lift_bias), t["fwd_y"], t["fwd_x"], t["spread"],
    )
    for layer in range(LAYERS):
        got = lax.all_to_all(out, "slab", split_axis=0, concat_axis=0, tiled=True)
        modes = call(
            functools.partial(modes_kernel, 1.0 / math.sqrt(slabs * depth)),
            jax.ShapeDtypeStruct((2, width, owned * K), bf),
            [pltpu.VMEM((owned // half * 2, width * half, half * K), bf)],
            got, t["fwd_z"], t["tile"], t["total"],
        )
        modes = lax.all_gather(modes, "section", axis=0)
        mixed = call(
            mix_body, jax.ShapeDtypeStruct((sections, 2, width // sections, owned * K), bf), [],
            modes, spectral_weight[layer],
        )
        mixed = lax.all_to_all(mixed, "section", split_axis=0, concat_axis=0, tiled=True)
        planes = call(
            planes_body, spec, [local], mixed, t["expand"], t["back_z"], t["leave"],
        )
        got = lax.all_to_all(planes, "slab", split_axis=0, concat_axis=0, tiled=True)
        if layer < LAYERS - 1:
            hidden, out = call(
                layer_kernel, (hid, spec), [kron, direct, local], got, hidden,
                bypass_weight[layer], bias[layer], t["collect"], t["back_x"], t["back_y"],
                t["fwd_y"], t["fwd_x"], t["spread"],
            )
        else:
            hidden = call(
                last_kernel, hid, [kron, direct, local], got, hidden,
                bypass_weight[layer], bias[layer], t["collect"], t["back_x"], t["back_y"],
            )
    return hidden[None]


def solution(mesh):
    slabs, sections = mesh.shape["slab"], mesh.shape["section"]
    placed = (
        P("section", None, "slab", None, None),
        P(),
        P(),
        P(None, None, None, "section", "slab"),
        P(),
        P(),
    )
    fits = 2 * K % slabs == 0

    def whole(fields, *rest):
        single = fits and fields.shape[0] == sections
        return jax.shard_map(
            on_device_fast if single else on_device,
            mesh=mesh,
            in_specs=placed,
            out_specs=P("section", None, "slab", None, None),
            check_vma=False,
        )(fields, *rest)

    return whole
```

profile of v0, /device:TPU:0, one launch (start us, length us, event | category | flops | bytes accessed | tf_op | source)
XLA Modules:
  0.0 141.8 jit_solution(9087816773161371030)
XLA Ops:
  0.8 0.9 copy-done.10
  1.7 0.9 copy-done.16
  4.1 7.4 %shard_map.172 = (bf16[32,2,128,128]{3,2,1,0:T(8,128)(2,1)S(1)}, bf16[1024,128]{1,0:T(8,128)(2,1)}) custom-call(bf16[4,2,128,128]{3,2,1,0:T(8,128)(2,1)S(1)} %bitcast.31, bf16[4,32]{1,0:T(4,128)(2,1)S(1)} %copy-done.20, f32[32,1,128]{2,1,0:T(1,128)S(1)} %broadcast_in_dim.21.lift_bias, bf16[512,256]{1,0:T(8,128)(2,1)S(1)} %copy-done.10, ...), custom_call_target="tpu_custom_call" | custom-call | tf_op jit(solution)/shard_map/pallas_call | solution.py:337
  11.5 1.3 copy-done.6
  12.8 7.4 %all-to-all-start = ((bf16[16,64,128]{2,1,0:T(8,128)(2,1)}), bf16[16,64,128]{2,1,0:T(8,128)(2,1)S(1)}, u32[]{:S(2)}, u32[]{:S(2)}) async-start(bf16[16,64,128]{2,1,0:T(8,128)(2,1)} %bitcast.1), calls=%async_computation | async-start | bytes 524288 | tf_op jit(solution)/shard_map/all_to_all | solution.py:372
  20.2 5.2 %slice_bitcast_fusion = (bf16[2,32,16,1024]{3,2,1,0:T(8,128)(2,1)}, bf16[2,32,16,1024]{3,2,1,0:T(8,128)(2,1)}) fusion(bf16[2,2,32,16,1024]{4,3,2,1,0:T(8,128)(2,1)} %param.21), kind=kLoop, calls=%fused_computation | loop fusion | bytes 8388608 | tf_op jit(solution)/shard_map/squeeze | solution.py:382
  25.5 4.8 %all-to-all-done = bf16[16,64,128]{2,1,0:T(8,128)(2,1)S(1)} async-done(((bf16[16,64,128]{2,1,0:T(8,128)(2,1)}), bf16[16,64,128]{2,1,0:T(8,128)(2,1)S(1)}, u32[]{:S(2)}, u32[]{:S(2)}) %all-to-all-start) | async-done | bytes 262176 | tf_op jit(solution)/shard_map/all_to_all | solution.py:372
  30.3 2.6 %shard_map.173 = bf16[2,32,1024]{2,1,0:T(8,128)(2,1)S(1)} custom-call(bf16[1024,128]{1,0:T(8,128)(2,1)S(1)} %bitcast.25, bf16[512,1024]{1,0:T(8,128)(2,1)S(1)} %copy-done.3, bf16[128,4096]{1,0:T(8,128)(2,1)S(1)} %copy-done.4, bf16[32,1024]{1,0:T(8,128)(2,1)S(1)} %copy-done.17), custom_call_target="tpu_custom_call" | custom-call | tf_op jit(solution)/shard_map/pallas_call | solution.py:337
  32.9 6.1 %all-gather = bf16[4,32,1024]{2,1,0:T(8,128)(2,1)S(1)} all-gather(bf16[2,32,1024]{2,1,0:T(8,128)(2,1)S(1)} %shard_map.173), channel_id=2, replica_groups=mesh['section'=2,'slab'=16] {'section'}, dimensions={0}, use_global_device_ids=true | all-gather | bytes 393216 | tf_op jit(solution)/shard_map/all_gather | solution.py:379
  39.0 1.5 %shard_map.174 = bf16[2,2,16,1024]{3,2,1,0:T(8,128)(2,1)S(1)} custom-call(bf16[2,2,32,1024]{3,2,1,0:T(8,128)(2,1)S(1)} %bitcast.29, bf16[2,32,16,1024]{3,2,1,0:T(8,128)(2,1)S(1)} %copy-done.2), custom_call_target="tpu_custom_call" | custom-call | tf_op jit(solution)/shard_map/pallas_call | solution.py:337
  40.5 7.2 %all_to_all.54.mixed = bf16[2,2,16,1024]{3,2,1,0:T(8,128)(2,1)S(1)} all-to-all(bf16[2,2,16,1024]{3,2,1,0:T(8,128)(2,1)S(1)} %shard_map.174), channel_id=1, replica_groups=mesh['section'=2,'slab'=16] {'section'}, dimensions={0} | all-to-all | bytes 262144 | tf_op jit(solution)/shard_map/all_to_all | solution.py:384
  47.7 4.1 %shard_map.175 = bf16[1024,128]{1,0:T(8,128)(2,1)S(1)} custom-call(bf16[2,2,16,1024]{3,2,1,0:T(8,128)(2,1)S(1)} %all_to_all.54.mixed, bf16[1024,32]{1,0:T(8,128)(2,1)S(1)} %copy-done.7, bf16[1024,64]{1,0:T(8,128)(2,1)S(1)} %copy-done.8, bf16[1024,1024]{1,0:T(8,128)(2,1)S(1)} %copy-done), custom_call_target="tpu_custom_call" | custom-call | tf_op jit(solution)/shard_map/pallas_call | solution.py:337
  52.5 4.4 %all-to-all-start.2 = ((bf16[16,64,128]{2,1,0:T(8,128)(2,1)}), bf16[16,64,128]{2,1,0:T(8,128)(2,1)}, u32[]{:S(2)}, u32[]{:S(2)}) async-start(bf16[16,64,128]{2,1,0:T(8,128)(2,1)} %bitcast.24), calls=%async_computation.2 | async-start | bytes 524288 | tf_op jit(solution)/shard_map/all_to_all | solution.py:388
  58.2 8.6 %all-to-all-done.2 = bf16[16,64,128]{2,1,0:T(8,128)(2,1)} async-done(((bf16[16,64,128]{2,1,0:T(8,128)(2,1)}), bf16[16,64,128]{2,1,0:T(8,128)(2,1)}, u32[]{:S(2)}, u32[]{:S(2)}) %all-to-all-start.2) | async-done | bytes 262176 | tf_op jit(solution)/shard_map/all_to_all | solution.py:388
  68.5 0.9 copy-done.13
  70.2 14.1 %shard_map.176 = (bf16[32,2,128,128]{3,2,1,0:T(8,128)(2,1)S(1)}, bf16[1024,128]{1,0:T(8,128)(2,1)S(1)}) custom-call(bf16[1024,128]{1,0:T(8,128)(2,1)} %bitcast.6.got, bf16[32,2,128,128]{3,2,1,0:T(8,128)(2,1)} %copy-done.6, bf16[32,32]{1,0:T(8,128)(2,1)S(1)} %get-tuple-element.16.weight, f32[32,1,128]{2,1,0:T(1,128)S(1)} %broadcast_in_dim.23.bias, ...), custom_call_target="tpu_custom_call" | custom-call | tf_op jit(solution)/shard_map/pallas_call | solution.py:337
  84.3 12.9 %all_to_all.55 = bf16[16,64,128]{2,1,0:T(8,128)(2,1)S(1)} all-to-all(bf16[16,64,128]{2,1,0:T(8,128)(2,1)S(1)} %bitcast.32), channel_id=1, replica_groups=mesh['section'=2,'slab'=16] {'slab'}, dimensions={0} | all-to-all | bytes 524288 | tf_op jit(solution)/shard_map/all_to_all | solution.py:372
  97.3 2.6 %shard_map.177 = bf16[2,32,1024]{2,1,0:T(8,128)(2,1)S(1)} custom-call(bf16[1024,128]{1,0:T(8,128)(2,1)S(1)} %bitcast.26, bf16[512,1024]{1,0:T(8,128)(2,1)S(1)} %copy-done.3, bf16[128,4096]{1,0:T(8,128)(2,1)S(1)} %copy-done.5, bf16[32,1024]{1,0:T(8,128)(2,1)S(1)} %copy-done.17), custom_call_target="tpu_custom_call" | custom-call | tf_op jit(solution)/shard_map/pallas_call | solution.py:337
  99.9 6.1 %all-gather.1 = bf16[4,32,1024]{2,1,0:T(8,128)(2,1)S(1)} all-gather(bf16[2,32,1024]{2,1,0:T(8,128)(2,1)S(1)} %shard_map.177), channel_id=3, replica_groups=mesh['section'=2,'slab'=16] {'section'}, dimensions={0}, use_global_device_ids=true | all-gather | bytes 393216 | tf_op jit(solution)/shard_map/all_gather | solution.py:379
  106.0 1.5 %shard_map.178 = bf16[2,2,16,1024]{3,2,1,0:T(8,128)(2,1)S(1)} custom-call(bf16[2,2,32,1024]{3,2,1,0:T(8,128)(2,1)S(1)} %bitcast.28, bf16[2,32,16,1024]{3,2,1,0:T(8,128)(2,1)S(1)} %copy-done.1), custom_call_target="tpu_custom_call" | custom-call | tf_op jit(solution)/shard_map/pallas_call | solution.py:337
  107.5 7.0 %all_to_all.56.mixed = bf16[2,2,16,1024]{3,2,1,0:T(8,128)(2,1)S(1)} all-to-all(bf16[2,2,16,1024]{3,2,1,0:T(8,128)(2,1)S(1)} %shard_map.178), channel_id=1, replica_groups=mesh['section'=2,'slab'=16] {'section'}, dimensions={0} | all-to-all | bytes 262144 | tf_op jit(solution)/shard_map/all_to_all | solution.py:384
  114.5 4.1 %shard_map.179 = bf16[1024,128]{1,0:T(8,128)(2,1)S(1)} custom-call(bf16[2,2,16,1024]{3,2,1,0:T(8,128)(2,1)S(1)} %all_to_all.56.mixed, bf16[1024,32]{1,0:T(8,128)(2,1)S(1)} %copy-done.7, bf16[1024,64]{1,0:T(8,128)(2,1)S(1)} %copy-done.9, bf16[1024,1024]{1,0:T(8,128)(2,1)S(1)} %copy-done), custom_call_target="tpu_custom_call" | custom-call | tf_op jit(solution)/shard_map/pallas_call | solution.py:337
  118.6 13.1 %all_to_all.57 = bf16[16,64,128]{2,1,0:T(8,128)(2,1)S(1)} all-to-all(bf16[16,64,128]{2,1,0:T(8,128)(2,1)S(1)} %bitcast.27), channel_id=1, replica_groups=mesh['section'=2,'slab'=16] {'slab'}, dimensions={0} | all-to-all | bytes 524288 | tf_op jit(solution)/shard_map/all_to_all | solution.py:388
  131.8 9.9 %shard_map.180 = bf16[32,2,128,128]{3,2,1,0:T(8,128)(2,1)} custom-call(bf16[1024,128]{1,0:T(8,128)(2,1)S(1)} %bitcast.30, bf16[32,2,128,128]{3,2,1,0:T(8,128)(2,1)S(1)} %get-tuple-element.12.hidden, bf16[32,32]{1,0:T(8,128)(2,1)S(1)} %get-tuple-element.15.weight, f32[32,1,128]{2,1,0:T(1,128)S(1)} %broadcast_in_dim.25.bias, ...), custom_call_target="tpu_custom_call" | custom-call | tf_op jit(solution)/shard_map/pallas_call | solution.py:337
  (48 shorter events, 6.7 us)
Async XLA Ops:
  0.8 1.0 copy-start.10
  1.7 0.9 copy-start.16
  2.7 0.8 copy-start.18
  11.5 1.3 copy-start.6
  12.8 17.4 %all-to-all-start = ((bf16[16,64,128]{2,1,0:T(8,128)(2,1)}), bf16[16,64,128]{2,1,0:T(8,128)(2,1)S(1)}, u32[]{:S(2)}, u32[]{:S(2)}) async-start(bf16[16,64,128]{2,1,0:T(8,128)(2,1)} %bitcast.1), calls=%async_computation | async-start | bytes 524288 | tf_op jit(solution)/shard_map/all_to_all | solution.py:372
  20.2 10.1 %copy-start.3 = (bf16[512,1024]{1,0:T(8,128)(2,1)S(1)}, bf16[512,1024]{1,0:T(8,128)(2,1)}, u32[]{:S(2)}) copy-start(bf16[512,1024]{1,0:T(8,128)(2,1)} %constant.28.clone.fwd_z) | copy-start | bytes 3145732
  20.2 10.0 %copy-start.4 = (bf16[128,4096]{1,0:T(8,128)(2,1)S(1)}, bf16[128,4096]{1,0:T(8,128)(2,1)}, u32[]{:S(2)}) copy-start(bf16[128,4096]{1,0:T(8,128)(2,1)} %constant.29.clone.tile) | copy-start | bytes 3145732
  20.2 10.0 %copy-start.17 = (bf16[32,1024]{1,0:T(8,128)(2,1)S(1)}, bf16[32,1024]{1,0:T(8,128)(2,1)}, u32[]{:S(2)}) copy-start(bf16[32,1024]{1,0:T(8,128)(2,1)} %constant.30.clone.total) | copy-start | bytes 196612
  30.3 8.7 %copy-start.2 = (bf16[2,32,16,1024]{3,2,1,0:T(8,128)(2,1)S(1)}, bf16[2,32,16,1024]{3,2,1,0:T(8,128)(2,1)}, u32[]{:S(2)}) copy-start(bf16[2,32,16,1024]{3,2,1,0:T(8,128)(2,1)} %get-tuple-element.14.weights) | copy-start | bytes 6291460
  32.9 14.8 %copy-start = (bf16[1024,1024]{1,0:T(8,128)(2,1)S(1)}, bf16[1024,1024]{1,0:T(8,128)(2,1)}, u32[]{:S(2)}) copy-start(bf16[1024,1024]{1,0:T(8,128)(2,1)} %constant.33.clone.leave) | copy-start | bytes 6291460
  32.9 14.8 %copy-start.7 = (bf16[1024,32]{1,0:T(8,128)(2,1)S(1)}, bf16[1024,32]{1,0:T(8,128)(2,1)}, u32[]{:S(2)}) copy-start(bf16[1024,32]{1,0:T(8,128)(2,1)} %constant.31.clone.expand) | copy-start | bytes 196612
  32.9 14.8 %copy-start.8 = (bf16[1024,64]{1,0:T(8,128)(2,1)S(1)}, bf16[1024,64]{1,0:T(8,128)(2,1)}, u32[]{:S(2)}) copy-start(bf16[1024,64]{1,0:T(8,128)(2,1)} %constant.32.clone.back_z) | copy-start | bytes 393220
  40.5 16.4 %copy-start.22 = (bf16[2,32]{1,0:T(2,128)(2,1)S(1)}, bf16[2,32]{1,0:T(2,128)(2,1)}, u32[]{:S(2)}) copy-start(bf16[2,32]{1,0:T(2,128)(2,1)} %param.23) | copy-start | bytes 388
  40.5 27.0 %copy-start.15 = (bf16[256,64]{1,0:T(8,128)(2,1)S(1)}, bf16[256,64]{1,0:T(8,128)(2,1)}, u32[]{:S(2)}) copy-start(bf16[256,64]{1,0:T(8,128)(2,1)} %constant.34.clone.back_x) | copy-start | bytes 98308
  51.8 0.7 copy-start.12
  52.5 14.3 %all-to-all-start.2 = ((bf16[16,64,128]{2,1,0:T(8,128)(2,1)}), bf16[16,64,128]{2,1,0:T(8,128)(2,1)}, u32[]{:S(2)}, u32[]{:S(2)}) async-start(bf16[16,64,128]{2,1,0:T(8,128)(2,1)} %bitcast.24), calls=%async_computation.2 | async-start | bytes 524288 | tf_op jit(solution)/shard_map/all_to_all | solution.py:388
  67.5 1.0 copy-start.11
  68.5 0.9 copy-start.13
  69.4 0.8 copy-start.19
  70.2 27.1 %copy-start.5 = (bf16[128,4096]{1,0:T(8,128)(2,1)S(1)}, bf16[128,4096]{1,0:T(8,128)(2,1)}, u32[]{:S(2)}) copy-start(bf16[128,4096]{1,0:T(8,128)(2,1)} %constant.29.clone.tile) | copy-start | bytes 3145732
  84.3 21.7 %copy-start.1 = (bf16[2,32,16,1024]{3,2,1,0:T(8,128)(2,1)S(1)}, bf16[2,32,16,1024]{3,2,1,0:T(8,128)(2,1)}, u32[]{:S(2)}) copy-start(bf16[2,32,16,1024]{3,2,1,0:T(8,128)(2,1)} %get-tuple-element.13.weights) | copy-start | bytes 6291460
  99.9 14.6 %copy-start.9 = (bf16[1024,64]{1,0:T(8,128)(2,1)S(1)}, bf16[1024,64]{1,0:T(8,128)(2,1)}, u32[]{:S(2)}) copy-start(bf16[1024,64]{1,0:T(8,128)(2,1)} %constant.32.clone.back_z) | copy-start | bytes 393220
  107.5 24.3 %copy-start.21 = (f32[32]{0:T(128)S(1)}, f32[32]{0:T(128)}, u32[]{:S(2)}) copy-start(f32[32]{0:T(128)} %get-tuple-element.17) | copy-start | bytes 388
  107.5 24.4 %copy-start.14 = (bf16[256,512]{1,0:T(8,128)(2,1)S(1)}, bf16[256,512]{1,0:T(8,128)(2,1)}, u32[]{:S(2)}) copy-start(bf16[256,512]{1,0:T(8,128)(2,1)} %constant.35.clone.back_y) | copy-start | bytes 786436
  (1 other events, 0.7 us)
where the time goes:
time: 143 us; the launch traced here: 142 us
  blocking collectives  52.4 us (37%)
  Pallas kernels  47.9 us (33%)
  local copies, waits for them, and re-layouts  16.1 us (11%)
  waiting for transfers between devices  13.4 us (9%)
  starting transfers between devices  11.8 us (8%)
    pallas_call x9, Pallas kernels, call(): pl.pallas_call(kernel, out_shape=outs, in_specs=[pl.BlockSpec(memory_spac...  47.9 us
    all_to_all x2, blocking collectives, on_device_fast(): lax.all_to_all(mixed, 'section', split_axis=0, concat_axis=0, tiled=True)  14.1 us
    all_to_all x1, blocking collectives, on_device_fast(): lax.all_to_all(planes, 'slab', split_axis=0, concat_axis=0, tiled=True)  13.1 us
    all_to_all x1, blocking collectives, on_device_fast(): got = lax.all_to_all(out, 'slab', split_axis=0, concat_axis=0, tiled=True)  12.9 us
    all_gather x2, blocking collectives, on_device_fast(): modes = lax.all_gather(modes, 'section', axis=0)  12.1 us
    all_to_all x1, waiting for transfers between devices, on_device_fast(): lax.all_to_all(planes, 'slab', split_axis=0, concat_axis=0, tiled=True)  8.61 us
    unnamed x46, local copies, waits for them, and re-layouts  8.13 us
    all_to_all x1, starting transfers between devices, on_device_fast(): got = lax.all_to_all(out, 'slab', split_axis=0, concat_axis=0, tiled=True)  7.38 us
  transfers between devices with their start and end apart: 2, of which 2 were waited for; matrix products, arithmetic and copies ran while one was open for 5% of the time, Pallas kernels for 0%

commit v1 on v0

--- a/solution.py
+++ b/solution.py
@@ -312,11 +312,6 @@
     forward_body(hidden, fwd_y, fwd_x, spread, local, out)
 
 
-def modes_kernel(scale, got, fwd_z, tile, total, modes, held):
-    place = lax.axis_index("slab")
-    modes_body(place, got, fwd_z, tile, total, modes, held, scale)
-
-
 def layer_kernel(
     got, hidden, weight, bias, collect, back_x, back_y, fwd_y, fwd_x, spread,
     new, out, kron, direct, local,
@@ -340,8 +335,133 @@
         in_specs=[pl.BlockSpec(memory_space=pltpu.VMEM)] * len(args),
         out_specs=jax.tree.map(lambda _: pl.BlockSpec(memory_space=pltpu.VMEM), outs),
         scratch_shapes=scratch,
-        compiler_params=pltpu.CompilerParams(vmem_limit_bytes=50 * 1024 * 1024),
+        compiler_params=pltpu.CompilerParams(vmem_limit_bytes=28 * 1024 * 1024),
     )(*args)
+
+
+def exchange(source, target, rows, send, recv):
+    slabs = lax.axis_size("slab")
+    me = lax.axis_index("slab")
+    mine = pl.ds(pl.multiple_of(me * rows, rows), rows)
+    copies = []
+    for d in range(1, slabs):
+        to = lax.rem(me + d, slabs)
+        copies.append(
+            pltpu.make_async_remote_copy(
+                src_ref=source.at[pl.ds(pl.multiple_of(to * rows, rows), rows)],
+                dst_ref=target.at[mine],
+                send_sem=send.at[d],
+                recv_sem=recv.at[d],
+                device_id={"slab": to},
+                device_id_type=pl.DeviceIdType.MESH,
+            )
+        )
+        copies[-1].start()
+    target[mine, :] = source[mine, :]
+    for copy in copies:
+        copy.wait()
+
+
+def middle_kernel(
+    layer, scale, spec, weights, fwd_z, tile, total, expand, back_z, leave, out,
+    got, held, modes, wide, mixed, joined, local, planes, back,
+    weight_sem, send_a, recv_a, send_b, recv_b, send_c, recv_c, send_d, recv_d,
+):
+    slabs, sections = lax.axis_size("slab"), lax.axis_size("section")
+    me, section = lax.axis_index("slab"), lax.axis_index("section")
+    rows = spec.shape[0] // slabs
+    load = pltpu.make_async_copy(weights.at[layer], wide, weight_sem)
+    load.start()
+    barrier = pltpu.get_barrier_semaphore()
+    for d in range(1, slabs):
+        pl.semaphore_signal(
+            barrier, inc=1, device_id={"slab": lax.rem(me + d, slabs)},
+            device_id_type=pl.DeviceIdType.MESH,
+        )
+    for e in range(1, sections):
+        pl.semaphore_signal(
+            barrier, inc=1, device_id={"section": lax.rem(section + e, sections)},
+            device_id_type=pl.DeviceIdType.MESH,
+        )
+    pl.semaphore_wait(barrier, slabs + sections - 2)
+    exchange(spec, got, rows, send_a, recv_a)
+    modes_body(me, got, fwd_z, tile, total, modes.at[0], held, scale)
+    copies = []
+    for e in range(1, sections):
+        copies.append(
+            pltpu.make_async_remote_copy(
+                src_ref=modes.at[0],
+                dst_ref=modes.at[e],
+                send_sem=send_b.at[e],
+                recv_sem=recv_b.at[e],
+                device_id={"section": lax.rem(section + e, sections)},
+                device_id_type=pl.DeviceIdType.MESH,
+            )
+        )
+        copies[-1].start()
+    load.wait()
+    mix_body(modes.at[0:1], wide, mixed.at[0:1])
+    joined[section] = mixed[0]
+    for copy in copies:
+        copy.wait()
+    copies = []
+    for e in range(1, sections):
+        mix_body(modes.at[e : e + 1], wide, mixed.at[e : e + 1])
+        copies.append(
+            pltpu.make_async_remote_copy(
+                src_ref=mixed.at[e],
+                dst_ref=joined.at[section],
+                send_sem=send_c.at[e],
+                recv_sem=recv_c.at[e],
+                device_id={"section": lax.rem(section + sections - e, sections)},
+                device_id_type=pl.DeviceIdType.MESH,
+            )
+        )
+        copies[-1].start()
+    for copy in copies:
+        copy.wait()
+    planes_body(joined, expand, back_z, leave, planes, local)
+    exchange(planes, back, rows, send_d, recv_d)
+    out[...] = back[...]
+
+
+def middle(layer, spec, weights, t, slabs, sections, depth):
+    bf = jnp.bfloat16
+    _, _, width, outs, lanes = weights.shape
+    half = 2 * K
+    share = pltpu.VMEM(spec.shape, bf)
+    vmem = pl.BlockSpec(memory_space=pltpu.VMEM)
+    tables = [t[name] for name in ("fwd_z", "tile", "total", "expand", "back_z", "leave")]
+    dma = pltpu.SemaphoreType.DMA
+    return pl.pallas_call(
+        functools.partial(middle_kernel, layer, 1.0 / math.sqrt(slabs * depth)),
+        out_shape=jax.ShapeDtypeStruct(spec.shape, bf),
+        in_specs=[vmem, pl.BlockSpec(memory_space=pl.ANY)] + [vmem] * len(tables),
+        out_specs=vmem,
+        scratch_shapes=[
+            share,
+            pltpu.VMEM((lanes // (half * K) * 2, width * half, half * K), bf),
+            pltpu.VMEM((sections, 2, width, lanes), bf),
+            pltpu.VMEM((2, width, outs, lanes), bf),
+            pltpu.VMEM((sections, 2, outs, lanes), bf),
+            pltpu.VMEM((sections, 2, outs, lanes), bf),
+            share,
+            share,
+            share,
+            dma,
+            dma((slabs,)),
+            dma((slabs,)),
+            dma((sections,)),
+            dma((sections,)),
+            dma((sections,)),
+            dma((sections,)),
+            dma((slabs,)),
+            dma((slabs,)),
+        ],
+        compiler_params=pltpu.CompilerParams(
+            collective_id=layer, has_side_effects=True, vmem_limit_bytes=28 * 1024 * 1024
+        ),
+    )(spec, weights, *tables)
 
 
 def on_device_fast(fields, lift_weight, lift_bias, spectral_weight, bypass_weight, bypass_bias):
@@ -349,7 +469,6 @@
     _, inputs, depth, nx, ny = fields.shape
     width = lift_weight.shape[1]
     half = 2 * K
-    owned = half * half // slabs
     bf = jnp.bfloat16
     t = constants(slabs, depth, nx, ny, width)
     t = {name: jnp.asarray(value) for name, value in t.items()}
@@ -369,23 +488,7 @@
         fields[0], lift_weight, spread_bias(lift_bias), t["fwd_y"], t["fwd_x"], t["spread"],
     )
     for layer in range(LAYERS):
-        got = lax.all_to_all(out, "slab", split_axis=0, concat_axis=0, tiled=True)
-        modes = call(
-            functools.partial(modes_kernel, 1.0 / math.sqrt(slabs * depth)),
-            jax.ShapeDtypeStruct((2, width, owned * K), bf),
-            [pltpu.VMEM((owned // half * 2, width * half, half * K), bf)],
-            got, t["fwd_z"], t["tile"], t["total"],
-        )
-        modes = lax.all_gather(modes, "section", axis=0)
-        mixed = call(
-            mix_body, jax.ShapeDtypeStruct((sections, 2, width // sections, owned * K), bf), [],
-            modes, spectral_weight[layer],
-        )
-        mixed = lax.all_to_all(mixed, "section", split_axis=0, concat_axis=0, tiled=True)
-        planes = call(
-            planes_body, spec, [local], mixed, t["expand"], t["back_z"], t["leave"],
-        )
-        got = lax.all_to_all(planes, "slab", split_axis=0, concat_axis=0, tiled=True)
+        got = middle(layer, out, spectral_weight, t, slabs, sections, depth)
         if layer < LAYERS - 1:
             hidden, out = call(
                 layer_kernel, (hid, spec), [kron, direct, local], got, hidden,

time: 143 us -> 104 us (0.73)
  blocking collectives: 52.4 us -> 0 us
  Pallas kernels: 47.9 us -> 92.2 us
  waiting for transfers between devices: 13.4 us -> 0 us
  starting transfers between devices: 11.8 us -> 0 us
  local copies, waits for them, and re-layouts: 16.1 us -> 11.4 us
    pallas_call x0 -> x2, Pallas kernels: none -> 67.4 us  [middle(): pl.pallas_call(functools.partial(middle_kernel, layer, 1.0 / math.sqrt(sl...]
    all_to_all x4 -> x0, blocking collectives: 40.2 us -> none  [the longest x2 14.1 us: on_device_fast(): lax.all_to_all(mixed, 'section', split_axis=0, concat_axis=0, tiled=True)]
    pallas_call x9 -> x3, Pallas kernels: 47.9 us -> 24.8 us  [call(): pl.pallas_call(kernel, out_shape=outs, in_specs=[pl.BlockSpec(memory_spac...]
    all_to_all x2 -> x0, waiting for transfers between devices: 13.4 us -> none  [the longest x1 8.61 us: on_device_fast(): lax.all_to_all(planes, 'slab', split_axis=0, concat_axis=0, tiled=True)]
    all_gather x2 -> x0, blocking collectives: 12.1 us -> none  [on_device_fast(): modes = lax.all_gather(modes, 'section', axis=0)]
    all_to_all x2 -> x0, starting transfers between devices: 11.8 us -> none  [the longest x1 7.38 us: on_device_fast(): got = lax.all_to_all(out, 'slab', split_axis=0, concat_axis=0, tiled=True)]
    squeeze x1 -> x0, local copies, waits for them, and re-layouts: 5.21 us -> none  [on_device_fast(): spectral_weight[layer]]
    unnamed x46, local copies, waits for them, and re-layouts: 8.13 us -> 10.5 us
  transfers between devices with their start and end apart: 2 -> 0, of which waited for: 2 -> 0; matrix products, arithmetic and copies ran while one was open for 5% -> 0% of each run, Pallas kernels for 0% -> 0%
where the time goes in v1:
time: 104 us
  Pallas kernels  92.2 us (89%)
  local copies, waits for them, and re-layouts  11.4 us (11%)
    pallas_call x2, Pallas kernels, middle(): pl.pallas_call(functools.partial(middle_kernel, layer, 1.0 / math.sqrt(sl...  67.4 us
    pallas_call x3, Pallas kernels, call(): pl.pallas_call(kernel, out_shape=outs, in_specs=[pl.BlockSpec(memory_spac...  24.8 us
    unnamed x46, local copies, waits for them, and re-layouts  10.5 us

profile of v1, /device:TPU:0, one launch (start us, length us, event | category | flops | bytes accessed | tf_op | source)
XLA Modules:
  0.0 103.9 jit_solution(12987336932068323549)
XLA Ops:
  0.0 0.7 broadcast_in_dim.21.lift_bias
  0.8 0.0 copy-start.2
  0.8 1.6 %copy-done.2 = bf16[1024,1024]{1,0:T(8,128)(2,1)S(1)} copy-done((bf16[1024,1024]{1,0:T(8,128)(2,1)S(1)}, bf16[1024,1024]{1,0:T(8,128)(2,1)}, u32[]{:S(2)}) %copy-start.2) | copy-done | bytes 2097176
  2.4 0.9 copy-done.10
  3.3 0.9 copy-done.17
  4.3 0.8 copy-done.18
  5.0 0.7 copy-done.20
  5.7 5.1 %shard_map.172 = (bf16[32,2,128,128]{3,2,1,0:T(8,128)(2,1)S(1)}, bf16[1024,128]{1,0:T(8,128)(2,1)S(1)}) custom-call(bf16[4,2,128,128]{3,2,1,0:T(8,128)(2,1)S(1)} %bitcast.10, bf16[4,32]{1,0:T(4,128)(2,1)S(1)} %copy-done.20, f32[32,1,128]{2,1,0:T(1,128)S(1)} %broadcast_in_dim.21.lift_bias, bf16[512,256]{1,0:T(8,128)(2,1)S(1)} %copy-done.10, ...), custom_call_target="tpu_custom_call" | custom-call | tf_op jit(solution)/shard_map/pallas_call | solution.py:332
  10.8 2.2 %copy-done = bf16[2,2,32,16,1024]{4,3,2,1,0:T(8,128)(2,1)S(1)} copy-done((bf16[2,2,32,16,1024]{4,3,2,1,0:T(8,128)(2,1)S(1)}, bf16[2,2,32,16,1024]{4,3,2,1,0:T(8,128)(2,1)}, u32[]{:S(2)}) %copy-start) | copy-done | bytes 4194328
  13.0 1.2 %copy-done.6 = bf16[512,1024]{1,0:T(8,128)(2,1)S(1)} copy-done((bf16[512,1024]{1,0:T(8,128)(2,1)S(1)}, bf16[512,1024]{1,0:T(8,128)(2,1)}, u32[]{:S(2)}) %copy-start.6) | copy-done | bytes 1048600
  14.2 1.2 %copy-done.8 = bf16[128,4096]{1,0:T(8,128)(2,1)S(1)} copy-done((bf16[128,4096]{1,0:T(8,128)(2,1)S(1)}, bf16[128,4096]{1,0:T(8,128)(2,1)}, u32[]{:S(2)}) %copy-start.8) | copy-done | bytes 1048600
  15.4 0.8 copy-done.16
  16.3 0.0 copy-start.11
  16.3 0.0 copy-start.14
  16.3 0.0 copy-start.15
  16.3 0.0 copy-start.19
  16.3 35.0 %shard_map.173.got = bf16[1024,128]{1,0:T(8,128)(2,1)S(1)} custom-call(bf16[1024,128]{1,0:T(8,128)(2,1)S(1)} %get-tuple-element.9.spec, bf16[2,2,32,16,1024]{4,3,2,1,0:T(8,128)(2,1)S(1)} %copy-done, bf16[512,1024]{1,0:T(8,128)(2,1)S(1)} %copy-done.6, bf16[128,4096]{1,0:T(8,128)(2,1)S(1)} %copy-done.8, bf16[32,1024]{1,0:T(8,128)(2,1)S(1)} %copy-done.16, ...), custom_call_target="tpu_custom_call" | custom-call | tf_op jit(solution)/shard_map/pallas_call | solution.py:436
  51.4 0.1 broadcast_in_dim.23.bias
  51.6 0.0 copy-start.7
  51.6 0.0 copy-start.9
  51.6 11.4 %shard_map.174 = (bf16[32,2,128,128]{3,2,1,0:T(8,128)(2,1)S(1)}, bf16[1024,128]{1,0:T(8,128)(2,1)S(1)}) custom-call(bf16[1024,128]{1,0:T(8,128)(2,1)S(1)} %shard_map.173.got, bf16[32,2,128,128]{3,2,1,0:T(8,128)(2,1)S(1)} %get-tuple-element.10.hidden, bf16[32,32]{1,0:T(8,128)(2,1)S(1)} %get-tuple-element.14.weight, f32[32,1,128]{2,1,0:T(1,128)S(1)} %broadcast_in_dim.23.bias, ...), custom_call_target="tpu_custom_call" | custom-call | tf_op jit(solution)/shard_map/pallas_call | solution.py:332
  63.0 32.4 %shard_map.175.got = bf16[1024,128]{1,0:T(8,128)(2,1)S(1)} custom-call(bf16[1024,128]{1,0:T(8,128)(2,1)S(1)} %get-tuple-element.11.spec, bf16[2,2,32,16,1024]{4,3,2,1,0:T(8,128)(2,1)S(1)} %copy-done.1, bf16[512,1024]{1,0:T(8,128)(2,1)S(1)} %copy-done.7, bf16[128,4096]{1,0:T(8,128)(2,1)S(1)} %copy-done.9, bf16[32,1024]{1,0:T(8,128)(2,1)S(1)} %copy-done.16, ...), custom_call_target="tpu_custom_call" | custom-call | tf_op jit(solution)/shard_map/pallas_call | solution.py:436
  95.4 0.1 broadcast_in_dim.25.bias
  95.5 8.4 %shard_map.176 = bf16[32,2,128,128]{3,2,1,0:T(8,128)(2,1)} custom-call(bf16[1024,128]{1,0:T(8,128)(2,1)S(1)} %shard_map.175.got, bf16[32,2,128,128]{3,2,1,0:T(8,128)(2,1)S(1)} %get-tuple-element.12.hidden, bf16[32,32]{1,0:T(8,128)(2,1)S(1)} %get-tuple-element.13.weight, f32[32,1,128]{2,1,0:T(1,128)S(1)} %broadcast_in_dim.25.bias, ...), custom_call_target="tpu_custom_call" | custom-call | tf_op jit(solution)/shard_map/pallas_call | solution.py:332
  (33 shorter events, 0.1 us)
Async XLA Ops:
  0.8 1.6 %copy-start.2 = (bf16[1024,1024]{1,0:T(8,128)(2,1)S(1)}, bf16[1024,1024]{1,0:T(8,128)(2,1)}, u32[]{:S(2)}) copy-start(bf16[1024,1024]{1,0:T(8,128)(2,1)} %constant.26.clone.spread) | copy-start | bytes 6291460
  2.3 0.9 copy-start.10
  3.3 0.9 copy-start.17
  4.2 0.8 copy-start.18
  5.0 0.7 copy-start.20
  5.7 5.1 %copy-start.5 = (bf16[1024,1024]{1,0:T(8,128)(2,1)S(1)}, bf16[1024,1024]{1,0:T(8,128)(2,1)}, u32[]{:S(2)}) copy-start(bf16[1024,1024]{1,0:T(8,128)(2,1)} %constant.33.clone.leave) | copy-start | bytes 6291460
  5.7 5.1 %copy-start.12 = (bf16[1024,32]{1,0:T(8,128)(2,1)S(1)}, bf16[1024,32]{1,0:T(8,128)(2,1)}, u32[]{:S(2)}) copy-start(bf16[1024,32]{1,0:T(8,128)(2,1)} %constant.31.clone.expand) | copy-start | bytes 196612
  5.7 5.1 %copy-start.13 = (bf16[1024,64]{1,0:T(8,128)(2,1)S(1)}, bf16[1024,64]{1,0:T(8,128)(2,1)}, u32[]{:S(2)}) copy-start(bf16[1024,64]{1,0:T(8,128)(2,1)} %constant.32.clone.back_z) | copy-start | bytes 393220
  10.8 2.2 %copy-start = (bf16[2,2,32,16,1024]{4,3,2,1,0:T(8,128)(2,1)S(1)}, bf16[2,2,32,16,1024]{4,3,2,1,0:T(8,128)(2,1)}, u32[]{:S(2)}) copy-start(bf16[2,2,32,16,1024]{4,3,2,1,0:T(8,128)(2,1)} %weights.3) | copy-start | bytes 12582916
  13.0 1.2 %copy-start.6 = (bf16[512,1024]{1,0:T(8,128)(2,1)S(1)}, bf16[512,1024]{1,0:T(8,128)(2,1)}, u32[]{:S(2)}) copy-start(bf16[512,1024]{1,0:T(8,128)(2,1)} %constant.28.clone.fwd_z) | copy-start | bytes 3145732
  14.2 1.2 %copy-start.8 = (bf16[128,4096]{1,0:T(8,128)(2,1)S(1)}, bf16[128,4096]{1,0:T(8,128)(2,1)}, u32[]{:S(2)}) copy-start(bf16[128,4096]{1,0:T(8,128)(2,1)} %constant.29.clone.tile) | copy-start | bytes 3145732
  15.4 0.8 copy-start.16
  16.3 35.0 %copy-start.22 = (bf16[2,32]{1,0:T(2,128)(2,1)S(1)}, bf16[2,32]{1,0:T(2,128)(2,1)}, u32[]{:S(2)}) copy-start(bf16[2,32]{1,0:T(2,128)(2,1)} %param.23) | copy-start | bytes 388
  16.3 35.2 %copy-start.21 = (bf16[2,32,32]{2,1,0:T(8,128)(2,1)S(1)}, bf16[2,32,32]{2,1,0:T(8,128)(2,1)}, u32[]{:S(2)}) copy-start(bf16[2,32,32]{2,1,0:T(8,128)(2,1)} %param.22) | copy-start | bytes 12292
  16.3 35.2 %copy-start.3 = (bf16[1024,1024]{1,0:T(8,128)(2,1)S(1)}, bf16[1024,1024]{1,0:T(8,128)(2,1)}, u32[]{:S(2)}) copy-start(bf16[1024,1024]{1,0:T(8,128)(2,1)} %constant.26.clone.spread) | copy-start | bytes 6291460
  16.3 35.2 %copy-start.4 = (bf16[1024,1024]{1,0:T(8,128)(2,1)S(1)}, bf16[1024,1024]{1,0:T(8,128)(2,1)}, u32[]{:S(2)}) copy-start(bf16[1024,1024]{1,0:T(8,128)(2,1)} %constant.27.clone.collect) | copy-start | bytes 6291460
  16.3 35.2 %copy-start.11 = (bf16[512,256]{1,0:T(8,128)(2,1)S(1)}, bf16[512,256]{1,0:T(8,128)(2,1)}, u32[]{:S(2)}) copy-start(bf16[512,256]{1,0:T(8,128)(2,1)} %constant.24.clone.fwd_y) | copy-start | bytes 786436
  16.3 35.2 %copy-start.14 = (bf16[256,512]{1,0:T(8,128)(2,1)S(1)}, bf16[256,512]{1,0:T(8,128)(2,1)}, u32[]{:S(2)}) copy-start(bf16[256,512]{1,0:T(8,128)(2,1)} %constant.35.clone.back_y) | copy-start | bytes 786436
  16.3 35.2 %copy-start.15 = (bf16[256,64]{1,0:T(8,128)(2,1)S(1)}, bf16[256,64]{1,0:T(8,128)(2,1)}, u32[]{:S(2)}) copy-start(bf16[256,64]{1,0:T(8,128)(2,1)} %constant.34.clone.back_x) | copy-start | bytes 98308
  16.3 35.2 %copy-start.19 = (bf16[64,256]{1,0:T(8,128)(2,1)S(1)}, bf16[64,256]{1,0:T(8,128)(2,1)}, u32[]{:S(2)}) copy-start(bf16[64,256]{1,0:T(8,128)(2,1)} %constant.25.clone.fwd_x) | copy-start | bytes 98308
  51.5 11.4 %copy-start.1 = (bf16[2,2,32,16,1024]{4,3,2,1,0:T(8,128)(2,1)S(1)}, bf16[2,2,32,16,1024]{4,3,2,1,0:T(8,128)(2,1)}, u32[]{:S(2)}) copy-start(bf16[2,2,32,16,1024]{4,3,2,1,0:T(8,128)(2,1)} %weights.3) | copy-start | bytes 12582916
  51.6 11.4 %copy-start.7 = (bf16[512,1024]{1,0:T(8,128)(2,1)S(1)}, bf16[512,1024]{1,0:T(8,128)(2,1)}, u32[]{:S(2)}) copy-start(bf16[512,1024]{1,0:T(8,128)(2,1)} %constant.28.clone.fwd_z) | copy-start | bytes 3145732
  51.6 11.4 %copy-start.9 = (bf16[128,4096]{1,0:T(8,128)(2,1)S(1)}, bf16[128,4096]{1,0:T(8,128)(2,1)}, u32[]{:S(2)}) copy-start(bf16[128,4096]{1,0:T(8,128)(2,1)} %constant.29.clone.tile) | copy-start | bytes 3145732

commit v2 on v1

--- a/solution.py
+++ b/solution.py
@@ -363,8 +363,8 @@
 
 
 def middle_kernel(
-    layer, scale, spec, weights, fwd_z, tile, total, expand, back_z, leave, out,
-    got, held, modes, wide, mixed, joined, local, planes, back,
+    layer, scale, spec, weights, fwd_z_in, tile_in, total_in, expand_in, back_z_in, leave_in, out,
+    fwd_z, tile, total, expand, back_z, leave, table_sem, got, held, modes, wide, mixed, joined, local, planes, back,
     weight_sem, send_a, recv_a, send_b, recv_b, send_c, recv_c, send_d, recv_d,
 ):
     slabs, sections = lax.axis_size("slab"), lax.axis_size("section")
@@ -372,6 +372,16 @@
     rows = spec.shape[0] // slabs
     load = pltpu.make_async_copy(weights.at[layer], wide, weight_sem)
     load.start()
+    pairs = (
+        (fwd_z_in, fwd_z), (tile_in, tile), (total_in, total),
+        (expand_in, expand), (back_z_in, back_z), (leave_in, leave),
+    )
+    fetches = [
+        pltpu.make_async_copy(source, target, table_sem.at[n])
+        for n, (source, target) in enumerate(pairs)
+    ]
+    for fetch in fetches:
+        fetch.start()
     barrier = pltpu.get_barrier_semaphore()
     for d in range(1, slabs):
         pl.semaphore_signal(
@@ -385,6 +395,8 @@
         )
     pl.semaphore_wait(barrier, slabs + sections - 2)
     exchange(spec, got, rows, send_a, recv_a)
+    for fetch in fetches:
+        fetch.wait()
     modes_body(me, got, fwd_z, tile, total, modes.at[0], held, scale)
     copies = []
     for e in range(1, sections):
@@ -436,9 +448,11 @@
     return pl.pallas_call(
         functools.partial(middle_kernel, layer, 1.0 / math.sqrt(slabs * depth)),
         out_shape=jax.ShapeDtypeStruct(spec.shape, bf),
-        in_specs=[vmem, pl.BlockSpec(memory_space=pl.ANY)] + [vmem] * len(tables),
+        in_specs=[vmem] + [pl.BlockSpec(memory_space=pl.ANY)] * (1 + len(tables)),
         out_specs=vmem,
         scratch_shapes=[
+            *(pltpu.VMEM(table.shape, bf) for table in tables),
+            dma((len(tables),)),
             share,
             pltpu.VMEM((lanes // (half * K) * 2, width * half, half * K), bf),
             pltpu.VMEM((sections, 2, width, lanes), bf),

time: 104 us -> 105 us (level)
  no operation moved by 1% of the time
where the time goes in v2:
time: 105 us
  Pallas kernels  93.2 us (89%)
  local copies, waits for them, and re-layouts  11.4 us (11%)
    pallas_call x2, Pallas kernels, middle(): pl.pallas_call(functools.partial(middle_kernel, layer, 1.0 / math.sqrt(sl...  68.4 us
    pallas_call x3, Pallas kernels, call(): pl.pallas_call(kernel, out_shape=outs, in_specs=[pl.BlockSpec(memory_spac...  24.8 us
    unnamed x46, local copies, waits for them, and re-layouts  10.5 us

profile of v2, /device:TPU:0, one launch (start us, length us, event | category | flops | bytes accessed | tf_op | source)
XLA Modules:
  0.0 104.9 jit_solution(12955157278642802919)
XLA Ops:
  0.0 0.7 broadcast_in_dim.21.lift_bias
  0.8 0.0 copy-start.2
  0.8 1.6 %copy-done.2 = bf16[1024,1024]{1,0:T(8,128)(2,1)S(1)} copy-done((bf16[1024,1024]{1,0:T(8,128)(2,1)S(1)}, bf16[1024,1024]{1,0:T(8,128)(2,1)}, u32[]{:S(2)}) %copy-start.2) | copy-done | bytes 2097176
  2.4 0.9 copy-done.10
  3.3 0.9 copy-done.17
  4.3 0.8 copy-done.18
  5.0 0.7 copy-done.20
  5.7 5.1 %shard_map.172 = (bf16[32,2,128,128]{3,2,1,0:T(8,128)(2,1)S(1)}, bf16[1024,128]{1,0:T(8,128)(2,1)S(1)}) custom-call(bf16[4,2,128,128]{3,2,1,0:T(8,128)(2,1)S(1)} %bitcast.10, bf16[4,32]{1,0:T(4,128)(2,1)S(1)} %copy-done.20, f32[32,1,128]{2,1,0:T(1,128)S(1)} %broadcast_in_dim.21.lift_bias, bf16[512,256]{1,0:T(8,128)(2,1)S(1)} %copy-done.10, ...), custom_call_target="tpu_custom_call" | custom-call | tf_op jit(solution)/shard_map/pallas_call | solution.py:332
  10.8 2.2 %copy-done = bf16[2,2,32,16,1024]{4,3,2,1,0:T(8,128)(2,1)S(1)} copy-done((bf16[2,2,32,16,1024]{4,3,2,1,0:T(8,128)(2,1)S(1)}, bf16[2,2,32,16,1024]{4,3,2,1,0:T(8,128)(2,1)}, u32[]{:S(2)}) %copy-start) | copy-done | bytes 4194328
  13.0 1.2 %copy-done.6 = bf16[512,1024]{1,0:T(8,128)(2,1)S(1)} copy-done((bf16[512,1024]{1,0:T(8,128)(2,1)S(1)}, bf16[512,1024]{1,0:T(8,128)(2,1)}, u32[]{:S(2)}) %copy-start.6) | copy-done | bytes 1048600
  14.2 1.2 %copy-done.8 = bf16[128,4096]{1,0:T(8,128)(2,1)S(1)} copy-done((bf16[128,4096]{1,0:T(8,128)(2,1)S(1)}, bf16[128,4096]{1,0:T(8,128)(2,1)}, u32[]{:S(2)}) %copy-start.8) | copy-done | bytes 1048600
  15.4 0.8 copy-done.16
  16.3 0.0 copy-start.11
  16.3 0.0 copy-start.14
  16.3 0.0 copy-start.15
  16.3 0.0 copy-start.19
  16.3 35.5 %shard_map.173.got = bf16[1024,128]{1,0:T(8,128)(2,1)S(1)} custom-call(bf16[1024,128]{1,0:T(8,128)(2,1)S(1)} %get-tuple-element.9.spec, bf16[2,2,32,16,1024]{4,3,2,1,0:T(8,128)(2,1)S(1)} %copy-done, bf16[512,1024]{1,0:T(8,128)(2,1)S(1)} %copy-done.6, bf16[128,4096]{1,0:T(8,128)(2,1)S(1)} %copy-done.8, bf16[32,1024]{1,0:T(8,128)(2,1)S(1)} %copy-done.16, ...), custom_call_target="tpu_custom_call" | custom-call | tf_op jit(solution)/shard_map/pallas_call | solution.py:448
  51.9 0.1 broadcast_in_dim.23.bias
  52.0 0.0 copy-start.7
  52.1 0.0 copy-start.9
  52.1 11.4 %shard_map.174 = (bf16[32,2,128,128]{3,2,1,0:T(8,128)(2,1)S(1)}, bf16[1024,128]{1,0:T(8,128)(2,1)S(1)}) custom-call(bf16[1024,128]{1,0:T(8,128)(2,1)S(1)} %shard_map.173.got, bf16[32,2,128,128]{3,2,1,0:T(8,128)(2,1)S(1)} %get-tuple-element.10.hidden, bf16[32,32]{1,0:T(8,128)(2,1)S(1)} %get-tuple-element.14.weight, f32[32,1,128]{2,1,0:T(1,128)S(1)} %broadcast_in_dim.23.bias, ...), custom_call_target="tpu_custom_call" | custom-call | tf_op jit(solution)/shard_map/pallas_call | solution.py:332
  63.5 32.9 %shard_map.175.got = bf16[1024,128]{1,0:T(8,128)(2,1)S(1)} custom-call(bf16[1024,128]{1,0:T(8,128)(2,1)S(1)} %get-tuple-element.11.spec, bf16[2,2,32,16,1024]{4,3,2,1,0:T(8,128)(2,1)S(1)} %copy-done.1, bf16[512,1024]{1,0:T(8,128)(2,1)S(1)} %copy-done.7, bf16[128,4096]{1,0:T(8,128)(2,1)S(1)} %copy-done.9, bf16[32,1024]{1,0:T(8,128)(2,1)S(1)} %copy-done.16, ...), custom_call_target="tpu_custom_call" | custom-call | tf_op jit(solution)/shard_map/pallas_call | solution.py:448
  96.4 0.1 broadcast_in_dim.25.bias
  96.5 8.4 %shard_map.176 = bf16[32,2,128,128]{3,2,1,0:T(8,128)(2,1)} custom-call(bf16[1024,128]{1,0:T(8,128)(2,1)S(1)} %shard_map.175.got, bf16[32,2,128,128]{3,2,1,0:T(8,128)(2,1)S(1)} %get-tuple-element.12.hidden, bf16[32,32]{1,0:T(8,128)(2,1)S(1)} %get-tuple-element.13.weight, f32[32,1,128]{2,1,0:T(1,128)S(1)} %broadcast_in_dim.25.bias, ...), custom_call_target="tpu_custom_call" | custom-call | tf_op jit(solution)/shard_map/pallas_call | solution.py:332
  (33 shorter events, 0.1 us)
Async XLA Ops:
  0.8 1.6 %copy-start.2 = (bf16[1024,1024]{1,0:T(8,128)(2,1)S(1)}, bf16[1024,1024]{1,0:T(8,128)(2,1)}, u32[]{:S(2)}) copy-start(bf16[1024,1024]{1,0:T(8,128)(2,1)} %constant.26.clone.spread) | copy-start | bytes 6291460
  2.3 0.9 copy-start.10
  3.3 0.9 copy-start.17
  4.2 0.8 copy-start.18
  5.0 0.7 copy-start.20
  5.7 5.1 %copy-start.5 = (bf16[1024,1024]{1,0:T(8,128)(2,1)S(1)}, bf16[1024,1024]{1,0:T(8,128)(2,1)}, u32[]{:S(2)}) copy-start(bf16[1024,1024]{1,0:T(8,128)(2,1)} %constant.33.clone.leave_in) | copy-start | bytes 6291460
  5.7 5.1 %copy-start.12 = (bf16[1024,32]{1,0:T(8,128)(2,1)S(1)}, bf16[1024,32]{1,0:T(8,128)(2,1)}, u32[]{:S(2)}) copy-start(bf16[1024,32]{1,0:T(8,128)(2,1)} %constant.31.clone.expand_in) | copy-start | bytes 196612
  5.7 5.1 %copy-start.13 = (bf16[1024,64]{1,0:T(8,128)(2,1)S(1)}, bf16[1024,64]{1,0:T(8,128)(2,1)}, u32[]{:S(2)}) copy-start(bf16[1024,64]{1,0:T(8,128)(2,1)} %constant.32.clone.back_z_in) | copy-start | bytes 393220
  10.8 2.2 %copy-start = (bf16[2,2,32,16,1024]{4,3,2,1,0:T(8,128)(2,1)S(1)}, bf16[2,2,32,16,1024]{4,3,2,1,0:T(8,128)(2,1)}, u32[]{:S(2)}) copy-start(bf16[2,2,32,16,1024]{4,3,2,1,0:T(8,128)(2,1)} %weights.3) | copy-start | bytes 12582916
  13.0 1.2 %copy-start.6 = (bf16[512,1024]{1,0:T(8,128)(2,1)S(1)}, bf16[512,1024]{1,0:T(8,128)(2,1)}, u32[]{:S(2)}) copy-start(bf16[512,1024]{1,0:T(8,128)(2,1)} %constant.28.clone.fwd_z_in) | copy-start | bytes 3145732
  14.2 1.2 %copy-start.8 = (bf16[128,4096]{1,0:T(8,128)(2,1)S(1)}, bf16[128,4096]{1,0:T(8,128)(2,1)}, u32[]{:S(2)}) copy-start(bf16[128,4096]{1,0:T(8,128)(2,1)} %constant.29.clone.tile_in) | copy-start | bytes 3145732
  15.4 0.8 copy-start.16
  16.3 35.5 %copy-start.22 = (bf16[2,32]{1,0:T(2,128)(2,1)S(1)}, bf16[2,32]{1,0:T(2,128)(2,1)}, u32[]{:S(2)}) copy-start(bf16[2,32]{1,0:T(2,128)(2,1)} %param.23) | copy-start | bytes 388
  16.3 35.7 %copy-start.21 = (bf16[2,32,32]{2,1,0:T(8,128)(2,1)S(1)}, bf16[2,32,32]{2,1,0:T(8,128)(2,1)}, u32[]{:S(2)}) copy-start(bf16[2,32,32]{2,1,0:T(8,128)(2,1)} %param.22) | copy-start | bytes 12292
  16.3 35.7 %copy-start.3 = (bf16[1024,1024]{1,0:T(8,128)(2,1)S(1)}, bf16[1024,1024]{1,0:T(8,128)(2,1)}, u32[]{:S(2)}) copy-start(bf16[1024,1024]{1,0:T(8,128)(2,1)} %constant.26.clone.spread) | copy-start | bytes 6291460
  16.3 35.7 %copy-start.4 = (bf16[1024,1024]{1,0:T(8,128)(2,1)S(1)}, bf16[1024,1024]{1,0:T(8,128)(2,1)}, u32[]{:S(2)}) copy-start(bf16[1024,1024]{1,0:T(8,128)(2,1)} %constant.27.clone.collect) | copy-start | bytes 6291460
  16.3 35.7 %copy-start.11 = (bf16[512,256]{1,0:T(8,128)(2,1)S(1)}, bf16[512,256]{1,0:T(8,128)(2,1)}, u32[]{:S(2)}) copy-start(bf16[512,256]{1,0:T(8,128)(2,1)} %constant.24.clone.fwd_y) | copy-start | bytes 786436
  16.3 35.7 %copy-start.14 = (bf16[256,512]{1,0:T(8,128)(2,1)S(1)}, bf16[256,512]{1,0:T(8,128)(2,1)}, u32[]{:S(2)}) copy-start(bf16[256,512]{1,0:T(8,128)(2,1)} %constant.35.clone.back_y) | copy-start | bytes 786436
  16.3 35.7 %copy-start.15 = (bf16[256,64]{1,0:T(8,128)(2,1)S(1)}, bf16[256,64]{1,0:T(8,128)(2,1)}, u32[]{:S(2)}) copy-start(bf16[256,64]{1,0:T(8,128)(2,1)} %constant.34.clone.back_x) | copy-start | bytes 98308
  16.3 35.7 %copy-start.19 = (bf16[64,256]{1,0:T(8,128)(2,1)S(1)}, bf16[64,256]{1,0:T(8,128)(2,1)}, u32[]{:S(2)}) copy-start(bf16[64,256]{1,0:T(8,128)(2,1)} %constant.25.clone.fwd_x) | copy-start | bytes 98308
  52.0 11.4 %copy-start.1 = (bf16[2,2,32,16,1024]{4,3,2,1,0:T(8,128)(2,1)S(1)}, bf16[2,2,32,16,1024]{4,3,2,1,0:T(8,128)(2,1)}, u32[]{:S(2)}) copy-start(bf16[2,2,32,16,1024]{4,3,2,1,0:T(8,128)(2,1)} %weights.3) | copy-start | bytes 12582916
  52.0 11.4 %copy-start.7 = (bf16[512,1024]{1,0:T(8,128)(2,1)S(1)}, bf16[512,1024]{1,0:T(8,128)(2,1)}, u32[]{:S(2)}) copy-start(bf16[512,1024]{1,0:T(8,128)(2,1)} %constant.28.clone.fwd_z_in) | copy-start | bytes 3145732
  52.1 11.4 %copy-start.9 = (bf16[128,4096]{1,0:T(8,128)(2,1)S(1)}, bf16[128,4096]{1,0:T(8,128)(2,1)}, u32[]{:S(2)}) copy-start(bf16[128,4096]{1,0:T(8,128)(2,1)} %constant.29.clone.tile_in) | copy-start | bytes 3145732
